TPU v7x, 256 devices: a whole 4x4x8 slice. The times are simulated.
256 devices in a mesh: seq: 8 (over y, x_hi), dp: 32 (over x_lo, z, core).
Axes of the slice: x: 4 (x_hi: 2, x_lo: 2; x = x_hi * 2 + x_lo), y: 4, z: 8, core: 2. Of those that a mesh axis runs over, the one named last changes fastest.
Arguments:
- queries: bfloat16 [32, 2048, 2048], P('dp', 'seq'), may hold values from -150 to 150
- group_memory: bfloat16 [32, 2048, 2, 896], P('dp', 'seq'), may hold values from -160 to 160
- nb_shard: int32 [32, 32, 2, 128, 1], P('dp', 'seq'), may hold values from 0 to 31; in each aligned block of 1024 rows (0 to 1023, 1024 to 2047, ..., all dimensions but the last counted through in order) at most 48 rows name the same one
- nb_row: int32 [32, 32, 2, 128], P('dp', 'seq'), may hold values from 0 to 2047
- embed: bfloat16 [65536, 896], P('dp'), may hold values from -6 to 6
- w_query_enc: bfloat16 [896, 896], P(None, 'dp'), may hold values from -0.1875 to 0.1875
- w_out_enc: bfloat16 [896, 896], P(None, 'dp'), may hold values from -0.1875 to 0.1875
- w_kv_cca: bfloat16 [896, 4096], P(None, 'dp'), may hold values from -0.1875 to 0.1875
Outputs:
- cca_out: bfloat16 [32, 2048, 2048], P('dp', 'seq')
Inputs may be any that keep to these rules, and one draw needn't show every extreme that they name: `nb_shard`: in each aligned block of the 1024 neighbour tokens of one device, no value is named more than 48 times, a bound that some block reaches.
All inputs are finite; a program needn't handle non-finite values.
Results may differ from a plain program's by a relative error of at most 0.02.
The roundings to bfloat16 on the way count: a program that leaves them out, or rounds other values in their place, can miss the bound.
Values may be sent and summed in bfloat16 or wider, within the bound.
A program may use at most 128 MiB of HBM per device.

v0:
```python
import math

import jax
import jax.numpy as jnp
from jax import lax
from jax.sharding import PartitionSpec as P

GROUP = 64
ENC_HD = 64
HQ = 16
HD = 128
ENC_HEADS = 14


def shifted(array, axis, by):
    count = lax.axis_size(axis)
    pairs = [(i, i + by) for i in range(count) if 0 <= i + by < count]
    return lax.ppermute(array, axis, pairs)


def soft_weights(scores):
    return jax.nn.softmax(scores, axis=-1).astype(jnp.bfloat16)


def column_product(left_operand, weight_piece):
    return jnp.dot(left_operand, weight_piece, preferred_element_type=jnp.float32)


def shards(queries, group_memory, nb_shard, nb_row, embed, w_query_enc, w_out_enc, w_kv_cca):
    n_dp = lax.axis_size("dp")
    owners = nb_shard.reshape(-1)
    table_rows = nb_row.reshape(-1)
    count = owners.shape[0]
    capacity = 3 * count // (2 * n_dp)
    group_count = nb_row.shape[1]
    span = nb_row.shape[2] * nb_row.shape[3]
    enc_width = embed.shape[1]
    query_width = queries.shape[2]
    local_tokens = queries.shape[1]
    marks = (owners[:, None] == jnp.arange(n_dp, dtype=jnp.int32)[None, :]).astype(jnp.int32)
    slots = jnp.sum((jnp.cumsum(marks, axis=0) - 1) * marks, axis=1)
    places = owners * capacity + slots
    requests = (
        jnp.zeros((n_dp * capacity,), jnp.int32).at[places].set(table_rows).reshape(n_dp, capacity)
    )
    found = jnp.take(
        embed, lax.all_to_all(requests, "dp", split_axis=0, concat_axis=0, tiled=True), axis=0
    )
    returned = lax.all_to_all(found, "dp", split_axis=0, concat_axis=0, tiled=True)
    neighbour_rows = jnp.take(returned.reshape(n_dp * capacity, enc_width), places, axis=0)
    wide_rows = neighbour_rows.astype(jnp.float32)
    normed = (
        wide_rows * lax.rsqrt(jnp.mean(wide_rows * wide_rows, axis=-1, keepdims=True) + 1e-06)
    ).astype(jnp.bfloat16)
    enc_query = column_product(normed, lax.all_gather(w_query_enc, "dp", axis=1, tiled=True))
    enc_query = enc_query.astype(jnp.bfloat16)
    head_query = enc_query.reshape(group_count, span, ENC_HEADS, ENC_HD)
    group_mem = group_memory.reshape(group_count, GROUP, 2, ENC_HEADS, ENC_HD)
    scores = jnp.einsum(
        "cnhd,cmhd->chnm", head_query, group_mem[:, :, 0], preferred_element_type=jnp.float32
    ) * (1.0 / math.sqrt(ENC_HD))
    mixed_heads = jnp.einsum(
        "chnm,cmhd->cnhd",
        soft_weights(scores),
        group_mem[:, :, 1],
        preferred_element_type=jnp.float32,
    )
    mixed_heads = mixed_heads.astype(jnp.bfloat16).reshape(count, enc_width)
    projected = column_product(mixed_heads, lax.all_gather(w_out_enc, "dp", axis=1, tiled=True))
    encoded = (wide_rows + projected).astype(jnp.bfloat16)
    keys_values = jnp.dot(
        encoded,
        lax.all_gather(w_kv_cca, "dp", axis=1, tiled=True),
        preferred_element_type=jnp.float32,
    ).astype(jnp.bfloat16)
    edge_kv = shifted(keys_values[count - span :], "seq", 1)
    stacked = jnp.concatenate([edge_kv, keys_values], axis=0).reshape(
        group_count + 1, span, 2 * query_width
    )
    padded = jnp.concatenate(
        [
            jnp.zeros((1, query_width), jnp.bfloat16),
            queries[0],
            jnp.zeros((GROUP - 1, query_width), jnp.bfloat16),
        ],
        axis=0,
    )
    padded = padded.reshape(group_count + 1, GROUP, HQ, HD)
    cca_keys = stacked[:, :, :query_width].reshape(group_count + 1, span, HQ, HD)
    cca_values = stacked[:, :, query_width:].reshape(group_count + 1, span, HQ, HD)
    cca_scores = jnp.einsum(
        "bqhd,bkhd->bhqk", padded, cca_keys, preferred_element_type=jnp.float32
    ) * (1.0 / math.sqrt(HD))
    attended = jnp.einsum(
        "bhqk,bkhd->bqhd", soft_weights(cca_scores), cca_values, preferred_element_type=jnp.float32
    )
    attended = attended.astype(jnp.bfloat16).reshape((group_count + 1) * GROUP, query_width)
    return attended[1 : local_tokens + 1][None]


def solution(mesh):
    in_specs = (
        P("dp", "seq", None),
        P("dp", "seq", None, None),
        P("dp", "seq", None, None, None),
        P("dp", "seq", None, None),
        P("dp", None),
        P(None, "dp"),
        P(None, "dp"),
        P(None, "dp"),
    )
    out_specs = P("dp", "seq", None)
    return jax.shard_map(shards, mesh=mesh, in_specs=in_specs, out_specs=out_specs, check_vma=False)
```

profile of v0, /device:TPU:26, one launch (start us, length us, event | category | flops | bytes accessed | tf_op | source)
XLA Modules:
  0.0 379.9 jit_solution(15096180600094230807)
XLA Ops:
  9.4 9.0 %reduce-window.6 = s32[32,8,128]{2,1,0:T(8,128)S(1)} reduce-window(s32[32,8,128]{2,1,0:T(8,128)S(1)} %fusion.33, s32[]{:T(128)} %constant.19.clone.1), window={size=1x1x128 pad=0_0x0_0x127_0}, to_apply=%region_0.0 | reduce-window | flops 4161536 | bytes 262148 | tf_op jit(solution)/shard_map/reduce-window
  20.3 4.5 %scatter_custom_fusion = s32[1536]{0:T(1024)S(1)} fusion(s32[1024]{0:T(1024)S(1)} %bitcast.94, s32[1024]{0:T(1024)} %bitcast.97, s32[]{:T(128)} %constant.19.clone.1), kind=kCustom, calls=%fused_computation.57 | custom fusion | bytes 6656 | tf_op jit(solution)/shard_map/scatter | solution.py:44
  24.9 17.0 %all_to_all.20 = s32[32,1,48]{2,1,0:T(1,128)S(1)} all-to-all(s32[32,1,48]{2,1,0:T(1,128)S(1)} %all_to_all.13), channel_id=1, replica_groups=mesh['seq'=8,'dp'=32] {'dp'}, dimensions={0} | all-to-all | bytes 12288 | tf_op jit(solution)/shard_map/all_to_all | solution.py:47
  42.0 9.0 %gather_fusion = bf16[1536,896]{1,0:T(8,128)(2,1)S(1)} fusion(bf16[2048,896]{1,0:T(8,128)(2,1)} %param.12, s32[2048]{0:T(1024)S(1)} %pad_clamp_fusion), kind=kCustom, calls=%fused_computation | custom fusion | bytes 5511168 | tf_op jit(solution)/shard_map/jit(_take)/gather | solution.py:46
  51.1 2.0 broadcast_select_fusion
  53.0 5.3 %all-to-all-start.1 = ((bf16[32,48,896]{2,1,0:T(8,128)(2,1)}), bf16[32,48,896]{2,1,0:T(8,128)(2,1)S(1)}, u32[]{:S(2)}, u32[]{:S(2)}) async-start(bf16[32,48,896]{2,1,0:T(8,128)(2,1)} %broadcast_select_fusion), calls=%async_computation.1 | async-start | bytes 5505024 | tf_op jit(solution)/shard_map/all_to_all | solution.py:49
  58.3 3.6 copy.28
  61.9 4.1 %reshape.142 = bf16[4,64,2,14,64]{1,0,4,3,2:T(4,128)(2,1)} reshape(bf16[1,256,2,896]{1,3,2,0:T(8,128)(2,1)} %copy.28) | data formatting | bytes 1835008 | tf_op jit(solution)/shard_map/reshape | solution.py:58
  66.0 3.7 fusion.46
  69.7 2.3 copy.44
  72.0 8.4 %all-gather.8.cloned.1.call-done = bf16[32,28,896]{2,1,0:T(8,128)(2,1)} async-done(((bf16[1,28,896]{2,1,0:T(8,128)(2,1)}), bf16[32,28,896]{2,1,0:T(8,128)(2,1)}) %all-gather.8.cloned.1.call-update) | async-done | bytes 1605648 | tf_op jit(solution)/shard_map/all_gather | solution.py:55
  80.4 3.5 reshape.175
  84.0 71.3 %all-gather.10.cloned.1.call-done = bf16[32,28,896]{2,1,0:T(8,128)(2,1)} async-done(((bf16[1,28,896]{2,1,0:T(8,128)(2,1)}), bf16[32,28,896]{2,1,0:T(8,128)(2,1)}) %all-gather.10.cloned.1.call-update) | async-done | bytes 1605648 | tf_op jit(solution)/shard_map/all_gather | solution.py:69
  155.2 3.6 reshape.177
  158.8 5.3 %gather_fusion.1 = bf16[1024,896]{1,0:T(8,128)(2,1)} fusion(bf16[1536,896]{1,0:T(8,128)(2,1)S(1)} %bitcast.73, s32[1024]{0:T(1024)S(1)} %broadcast_clamp_fusion), kind=kCustom, calls=%fused_computation.1 | custom fusion | bytes 3674112 | tf_op jit(solution)/shard_map/jit(_take)/gather | solution.py:50
  164.1 2.2 fusion.5
  166.3 4.3 %fusion.21 = bf16[1024,896]{1,0:T(8,128)(2,1)S(1)} fusion(bf16[896,896]{1,0:T(8,128)(2,1)} %reshape.175, f32[1024]{0:T(1024)S(1)} %add_rsqrt_fusion, bf16[1024,896]{1,0:T(8,128)(2,1)} %gather_fusion.1, pred[1024]{0:T(1024)(128)(4,1)S(1)} %compare_and_fusion.1), kind=kOutput, calls=%fused_computation.32 | convolution fusion | flops 1648754688 | bytes 5280768 | tf_op jit(solution)/shard_map/dot_general | solution.py:26
  170.6 4.1 %reshape.178 = bf16[4,256,14,64]{3,2,1,0:T(8,128)(2,1)} reshape(bf16[1024,896]{1,0:T(8,128)(2,1)S(1)} %fusion.21) | data formatting | bytes 3670016 | tf_op jit(solution)/shard_map/reshape | solution.py:57
  174.7 3.6 fusion.8
  178.3 5.6 %fusion.47 = (f32[4,14,256]{2,1,0:T(8,128)S(1)}, f32[4,14,256,64]{2,3,1,0:T(8,128)S(1)}) fusion(f32[4,14,256,64]{2,3,1,0:T(8,128)S(1)} %fusion.8), kind=kOutput, calls=%fused_computation.68 | output fusion | flops 3670079 | bytes 7397376 | tf_op jit(solution)/shard_map/sub | solution.py:22
  187.8 54.0 %all-gather.6.cloned.1.call-done = bf16[896,4096]{1,0:T(8,128)(2,1)} async-done(((bf16[896,128]{1,0:T(8,128)(2,1)}), bf16[896,4096]{1,0:T(8,128)(2,1)}) %all-gather.6.cloned.1.call-update) | async-done | bytes 7340048 | tf_op jit(solution)/shard_map/all_gather | solution.py:73
  241.8 16.9 %convolution_convert_fusion = bf16[1024,4096]{1,0:T(8,128)(2,1)} fusion(bf16[896,4096]{1,0:T(8,128)(2,1)} %all-gather.6.cloned.1.call-done, bf16[1024,896]{0,1:T(8,128)(2,1)} %bitcast.82, bf16[896,896]{1,0:T(8,128)(2,1)S(1)} %copy-done.4, bf16[1024,896]{1,0:T(8,128)(2,1)S(1)} %copy-done.2, pred[1024]{0:T(1024)(128)(4,1)S(1)} %compare_and_fusion.1), kind=kOutput, calls=%fused_computation.6 | convolution fusion | flops 9168224256 | bytes 21005312 | tf_op jit(solution)/shard_map/dot_general | solution.py:71
  260.6 4.1 %collective-permute-start = (bf16[256,4096]{1,0:T(8,128)(2,1)S(1)}, bf16[256,4096]{1,0:T(8,128)(2,1)S(1)}, u32[]{:S(2)}, u32[]{:S(2)}) collective-permute-start(bf16[256,4096]{1,0:T(8,128)(2,1)S(1)} %slice.40), channel_id=1, source_target_pairs={{0,32},{32,64},{64,96},{96,128},{128,160},{160,192},{192,224},{1,3... | collective-permute-start | bytes 6291464 | tf_op jit(solution)/shard_map/ppermute | solution.py:18
  266.9 46.0 %collective-permute-done = bf16[256,4096]{1,0:T(8,128)(2,1)S(1)} collective-permute-done((bf16[256,4096]{1,0:T(8,128)(2,1)S(1)}, bf16[256,4096]{1,0:T(8,128)(2,1)S(1)}, u32[]{:S(2)}, u32[]{:S(2)}) %collective-permute-start) | collective-permute-done | bytes 2097184 | tf_op jit(solution)/shard_map/ppermute | solution.py:18
  312.9 9.8 %pad_maximum_fusion = bf16[1280,4096]{1,0:T(8,128)(2,1)} fusion(bf16[1024,4096]{1,0:T(8,128)(2,1)S(1)} %copy-done, bf16[256,4096]{1,0:T(8,128)(2,1)S(1)} %collective-permute-done), kind=kLoop, calls=%fused_computation.5 | loop fusion | flops 20971520 | bytes 20971520 | tf_op jit(solution)/shard_map/concatenate | solution.py:77
  322.7 10.2 %fusion.45 = (bf16[5,256,2048]{2,1,0:T(8,128)(2,1)}, bf16[5,256,2048]{2,1,0:T(8,128)(2,1)}) fusion(bf16[5,256,4096]{2,1,0:T(8,128)(2,1)} %bitcast.74), kind=kLoop, calls=%fused_computation.66 | loop fusion | bytes 20971520 | tf_op jit(solution)/shard_map/slice | solution.py:89
  332.9 7.8 %copy.46 = bf16[5,256,2048]{1,2,0:T(8,128)(2,1)} copy(bf16[5,256,2048]{2,1,0:T(8,128)(2,1)} %get-tuple-element.5) | data formatting | bytes 10485760
  340.7 3.3 fusion.26
  344.1 2.3 copy-done.1
  346.4 2.0 fusion.48
  348.4 7.8 %copy.45 = bf16[5,256,2048]{1,2,0:T(8,128)(2,1)} copy(bf16[5,256,2048]{2,1,0:T(8,128)(2,1)} %get-tuple-element.6) | data formatting | bytes 10485760
  356.2 14.6 %fusion.25 = bf16[5,64,16,128]{3,1,2,0:T(8,128)(2,1)S(1)} fusion(bf16[5,256,16,128]{1,3,2,0:T(8,128)(2,1)} %bitcast.79, f32[5,16,64]{2,1,0:T(8,128)S(1)} %fusion.48, f32[5,16,64,256]{3,2,1,0:T(8,128)} %copy-done.1), kind=kOutput, calls=%fused_computation.34 | convolution fusion | flops 342758656 | bytes 11816960 | tf_op jit(solution)/shard_map/bhqk,bkhd->bqhd/dot_general | solution.py:94
  (50 shorter events, 15.4 us)
Async XLA Ops:
  6.5 73.9 %all-gather.8.cloned.1.call-start = ((), (), s32[]{:S(2)}) async-start(), calls=%async_computation.3 | async-start | bytes 1892352 | tf_op jit(solution)/shard_map/all_gather | solution.py:55
  7.3 148.0 %all-gather.10.cloned.1.call-start = ((), (), s32[]{:S(2)}) async-start(), calls=%async_computation.4 | async-start | bytes 1892352 | tf_op jit(solution)/shard_map/all_gather | solution.py:69
  8.0 233.8 %all-gather.6.cloned.1.call-start = ((), (), s32[]{:S(2)}) async-start(), calls=%async_computation.2 | async-start | bytes 7569408 | tf_op jit(solution)/shard_map/all_gather | solution.py:73
  53.0 105.8 %all-to-all-start.1 = ((bf16[32,48,896]{2,1,0:T(8,128)(2,1)}), bf16[32,48,896]{2,1,0:T(8,128)(2,1)S(1)}, u32[]{:S(2)}, u32[]{:S(2)}) async-start(bf16[32,48,896]{2,1,0:T(8,128)(2,1)} %broadcast_select_fusion), calls=%async_computation.1 | async-start | bytes 5505024 | tf_op jit(solution)/shard_map/all_to_all | solution.py:49
  61.9 10.1 %copy-start.6 = (s32[1,4,2,128,1]{3,4,2,1,0:T(1,128)S(1)}, s32[1,4,2,128,1]{3,4,2,1,0:T(1,128)}, u32[]{:S(2)}) copy-start(s32[1,4,2,128,1]{3,4,2,1,0:T(1,128)} %param.10) | copy-start | bytes 12292
  170.6 4.1 %copy-start.3 = (bf16[4,64,1,14,64]{4,1,3,0,2:T(8,128)(2,1)S(1)}, bf16[4,64,1,14,64]{4,1,3,0,2:T(8,128)(2,1)}, u32[]{:S(2)}) copy-start(bf16[4,64,1,14,64]{4,1,3,0,2:T(8,128)(2,1)} %copy.44) | copy-start | bytes 1376260
  178.3 5.6 %copy-start.5 = (bf16[4,64,1,14,64]{1,0,4,3,2:T(4,128)(2,1)S(1)}, bf16[4,64,1,14,64]{1,0,4,3,2:T(4,128)(2,1)}, u32[]{:S(2)}) copy-start(bf16[4,64,1,14,64]{1,0,4,3,2:T(4,128)(2,1)} %get-tuple-element.7) | copy-start | bytes 1376260
  184.7 57.1 %copy-start.2 = (bf16[1024,896]{1,0:T(8,128)(2,1)S(1)}, bf16[1024,896]{1,0:T(8,128)(2,1)}, u32[]{:S(2)}) copy-start(bf16[1024,896]{1,0:T(8,128)(2,1)} %gather_fusion.1) | copy-start | bytes 5505028
  184.7 57.1 %copy-start.4 = (bf16[896,896]{1,0:T(8,128)(2,1)S(1)}, bf16[896,896]{1,0:T(8,128)(2,1)}, u32[]{:S(2)}) copy-start(bf16[896,896]{1,0:T(8,128)(2,1)} %reshape.177) | copy-start | bytes 4816900
  258.7 54.2 %copy-start = (bf16[1024,4096]{1,0:T(8,128)(2,1)S(1)}, bf16[1024,4096]{1,0:T(8,128)(2,1)}, u32[]{:S(2)}) copy-start(bf16[1024,4096]{1,0:T(8,128)(2,1)} %convolution_convert_fusion) | copy-start | bytes 25165828
  260.6 52.3 %collective-permute-start = (bf16[256,4096]{1,0:T(8,128)(2,1)S(1)}, bf16[256,4096]{1,0:T(8,128)(2,1)S(1)}, u32[]{:S(2)}, u32[]{:S(2)}) collective-permute-start(bf16[256,4096]{1,0:T(8,128)(2,1)S(1)} %slice.40), channel_id=1, source_target_pairs={{0,32},{32,64},{64,96},{96,128},{128,160},{160,192},{192,224},{1,3... | collective-permute-start | bytes 6291464 | tf_op jit(solution)/shard_map/ppermute | solution.py:18
  344.1 2.4 copy-start.1
Sparse Core Ops, SparseCore 0:
  9.2 71.1 all-gather.7
  82.3 72.9 all-gather.9
  157.0 84.7 all-gather.5
where the time goes:
time: 381 us; the launch traced here: 380 us
  waiting for transfers between devices  182 us (48%)
  local copies, waits for them, and re-layouts  80.2 us (21%)
  matrix products  43.4 us (11%)
  other arithmetic  34.7 us (9%)
  blocking collectives  17 us (4%)
  between operations  13.4 us (4%)
  starting transfers between devices  9.49 us (2%)
    all_gather x1, waiting for transfers between devices, shards(): lax.all_gather(w_out_enc, 'dp', axis=1, tiled=True)  71.3 us
    all_gather x1, waiting for transfers between devices, shards(): lax.all_gather(w_kv_cca, 'dp', axis=1, tiled=True)  54 us
    ppermute x1, waiting for transfers between devices, shifted(): return lax.ppermute(array, axis, pairs)  46 us
    unnamed x23, local copies, waits for them, and re-layouts  33.3 us
    all_to_all x1, blocking collectives, shards(): lax.all_to_all(requests, 'dp', split_axis=0, concat_axis=0, tiled=True)  17 us
    dot_general x1, matrix products, shards(): jnp.dot(encoded, lax.all_gather(w_kv_cca, 'dp', axis=1, tiled=True), pref...  16.9 us
    dot_general x1, matrix products, shards(): jnp.einsum('bhqk,bkhd->bqhd', soft_weights(cca_scores), cca_values, prefe...  14.6 us
    slice x1, local copies, waits for them, and re-layouts, shards(): stacked[:, :, :query_width].reshape(group_count + 1, span, HQ, HD)  10.2 us
  transfers between devices with their start and end apart: 5, of which 4 were waited for; matrix products, arithmetic and copies ran while one was open for 21% of the time, Pallas kernels for 0%

commit v1 on v0

v1 whole, which is shorter than its diff:
```python
import functools
import math

import jax
import jax.numpy as jnp
from jax import lax
from jax.experimental import pallas as pl
from jax.experimental.pallas import tpu as pltpu
from jax.sharding import PartitionSpec as P

MESH = pl.DeviceIdType.MESH
BF = jnp.bfloat16
F32 = jnp.float32
ENC = 896
QW = 2048
HQ = 16
HD = 128
CAP = 48
TOK = 1024
PAIRS = 7
UNITS = 4
UROWS = 384
SLOTS = 1536
NEG = -1e30


def nt(a, b):
    return lax.dot_general(a, b, (((1,), (1,)), ((), ())), preferred_element_type=F32)


def nn(a, b):
    return jnp.dot(a, b, preferred_element_type=F32)


def iota(shape, dim):
    return lax.broadcasted_iota(jnp.int32, shape, dim)


def offset_of(k):
    base = 4 - (k + 1) // 2
    odd = lax.rem(k, 2)
    return lax.rem(odd * base + (1 - odd) * (8 - base), 8)


def body(
    own_ref, rid_ref, emb_hbm, wq_ref, wo_ref, wkv_ref, gm_hbm, q_hbm,
    out_ref,
    emb, gm, q, packk, packq, gk, gq, send, rows, onehot, keys, valt, wqt, wot, pieces,
    kbd, vbd, reqs, rreqs, icol, gcol, gpos, xenc, qenc, mixed, qnext, fin, outp,
    lsem, zks, zkr, zqs, zqr, yks, ykr, yqs, yqr, xks, xkr, xqs, xqr, sks, skr, sqs, sqr,
    rs, rr, ts, tr, ns, nr, fs, fr,
):
    seq = lax.axis_index("seq")
    dp = lax.axis_index("dp")
    xl = dp // 16
    z = lax.rem(dp // 2, 8)
    c = lax.rem(dp, 2)
    y = seq // 2
    xh = lax.rem(seq, 2)
    x = xh * 2 + xl
    xo = 1 - xl

    def at_x(xx):
        return (y * 2 + xx // 2, lax.rem(xx, 2) * 16 + z * 2 + c)

    partner = at_x(x + 1 - 2 * xl)
    wrap = at_x(lax.rem(x + 3 + 2 * xl, 4))
    sib = (seq, xl * 16 + z * 2 + 1 - c)
    nxt = (lax.rem(seq + 1, 8), dp)
    prv = (lax.rem(seq + 7, 8), dp)

    c_emb = pltpu.make_async_copy(emb_hbm, emb, lsem.at[0])
    c_q = pltpu.make_async_copy(q_hbm, q, lsem.at[1])
    c_gm = pltpu.make_async_copy(gm_hbm, gm, lsem.at[2])
    c_emb.start()
    c_q.start()
    c_gm.start()

    bar = pltpu.get_barrier_semaphore()

    def greet(k, _):
        pl.semaphore_signal(bar, inc=1, device_id=(seq, lax.rem(dp + k, 32)), device_id_type=MESH)
        return 0

    lax.fori_loop(1, 32, greet, 0)
    for k in range(1, 4):
        pl.semaphore_signal(bar, inc=1, device_id=(lax.rem(y + k, 4) * 2 + xh, dp), device_id_type=MESH)
    for dev in (partner, wrap, nxt, prv):
        pl.semaphore_signal(bar, inc=1, device_id=dev, device_id_type=MESH)

    kvt = wkv_ref[...].T
    packk[...] = kvt.reshape(4, 32, ENC)
    zero4 = jnp.zeros((4, ENC), BF)
    packq[0] = wq_ref[0:16, :]
    packq[1] = jnp.concatenate([wq_ref[16:28, :].astype(F32), zero4.astype(F32)], axis=0).astype(BF)
    packq[2] = wo_ref[0:16, :]
    packq[3] = jnp.concatenate([wo_ref[16:28, :].astype(F32), zero4.astype(F32)], axis=0).astype(BF)

    pl.semaphore_wait(bar, 38)

    def rdma(src, dst, s, r, dev):
        return pltpu.make_async_remote_copy(
            src_ref=src, dst_ref=dst, send_sem=s, recv_sem=r, device_id=dev, device_id_type=MESH
        )

    KQ = (packq, gq, zqs, zqr, yqs, yqr, xqs, xqr, sqs, sqr)
    KK = (packk, gk, zks, zkr, yks, ykr, xks, xkr, sks, skr)

    def zcopy(kind, zz):
        pack, g, s, r = kind[0], kind[1], kind[2], kind[3]
        return rdma(pack.at[y], g.at[xl, c, z, y], s.at[zz], r.at[z], (seq, xl * 16 + zz * 2 + c))

    def zcopy_in(kind, zz):
        pack, g, s, r = kind[0], kind[1], kind[2], kind[3]
        return rdma(pack.at[y], g.at[xl, c, zz, y], s.at[zz], r.at[zz], (seq, xl * 16 + zz * 2 + c))

    def ycopy(kind, zz, yy):
        g, s, r = kind[1], kind[4], kind[5]
        p = g.at[xl, c, zz, y]
        return rdma(p, p, s.at[zz, yy], r.at[zz, y], (yy * 2 + xh, dp))

    def ycopy_in(kind, zz, yy):
        g, s, r = kind[1], kind[4], kind[5]
        p = g.at[xl, c, zz, yy]
        return rdma(p, p, s.at[zz, yy], r.at[zz, yy], (yy * 2 + xh, dp))

    def xcopy(kind, zz, dev):
        g, s, r = kind[1], kind[6], kind[7]
        p = g.at[xl, c, zz]
        return rdma(p, p, s.at[zz], r.at[zz], dev)

    def xcopy_in(kind, zz):
        g, s, r = kind[1], kind[6], kind[7]
        p = g.at[xo, c, zz]
        return rdma(p, p, s.at[zz], r.at[zz], partner)

    def scopy(kind, a, zz):
        g, s, r = kind[1], kind[8], kind[9]
        p = g.at[a, c, zz]
        return rdma(p, p, s.at[a, zz], r.at[a, zz], sib)

    def scopy_in(kind, a, zz):
        g, s, r = kind[1], kind[8], kind[9]
        p = g.at[a, 1 - c, zz]
        return rdma(p, p, s.at[a, zz], r.at[a, zz], sib)

    def loop(lo, hi, fn):
        def step(k, _):
            fn(k)
            return 0

        lax.fori_loop(lo, hi, step, 0)

    def z_send(kind):
        loop(1, 8, lambda k: zcopy(kind, lax.rem(z + k, 8)).start())

    def y_send(kind, lo, hi):
        def one(k):
            zz = lax.rem(z + k, 8)
            zcopy_in(kind, zz).wait_recv()
            for j in range(1, 4):
                ycopy(kind, zz, lax.rem(y + j, 4)).start()

        loop(lo, hi, one)

    def x_send(kind, lo, hi):
        def one(k):
            zz = lax.rem(z + k, 8)

            @pl.when(k > 0)
            def _():
                for j in range(1, 4):
                    ycopy_in(kind, zz, lax.rem(y + j, 4)).wait_recv()

            @pl.when(lax.rem(zz, 4) == 0)
            def _():
                xcopy(kind, zz, partner).start()

            @pl.when(lax.rem(zz, 4) != 0)
            def _():
                xcopy(kind, zz, wrap).start()

            scopy(kind, xl, zz).start()

        loop(lo, hi, one)

    def x_pass(kind, lo, hi):
        def one(k):
            zz = lax.rem(z + k, 8)
            xcopy_in(kind, zz).wait_recv()
            scopy(kind, xo, zz).start()

        loop(lo, hi, one)

    def s_wait(kind):
        def one(zz):
            for a in range(2):
                scopy_in(kind, a, zz).wait_recv()

        loop(0, 8, one)

    def drain(kind):
        def one(zz):
            xcopy(kind, zz, partner).wait_send()
            for a in range(2):
                scopy(kind, a, zz).wait_send()

        loop(0, 8, one)

        def two(k):
            zz = lax.rem(z + k, 8)
            zcopy(kind, zz).wait_send()
            for j in range(1, 4):
                ycopy(kind, zz, lax.rem(y + j, 4)).wait_send()

        loop(1, 8, two)

    z_send(KQ)
    z_send(KK)
    c_lq = pltpu.make_async_copy(packq, gq.at[xl, c, z], lsem.at[3])
    c_lk = pltpu.make_async_copy(packk, gk.at[xl, c, z], lsem.at[4])
    c_lq.start()
    c_lk.start()

    own = own_ref[...]
    marks = (iota((32, TOK), 0) == own).astype(F32)
    upper = (iota((128, 128), 0) <= iota((128, 128), 1)).astype(BF)
    total = jnp.zeros((32, 1), F32)
    parts = []
    for k in range(TOK // 128):
        m = marks[:, k * 128 : (k + 1) * 128]
        cum = nn(m.astype(BF), upper) + total
        total = cum[:, 127:128]
        parts.append(jnp.sum(m * (cum - 1.0), axis=0, keepdims=True))
    slot = jnp.concatenate(parts, axis=1).astype(jnp.int32)
    place = (iota((128, TOK), 0) == slot).astype(BF)
    rid = rid_ref[...]
    high = (rid // 64).astype(F32)
    low = (rid - (rid // 64) * 64).astype(F32)
    group = (iota((1, TOK), 1) // 256 + 1).astype(F32)
    hi = nt((marks * high).astype(BF), place)
    lo = nt((marks * low).astype(BF), place)
    asked = (hi * 64.0 + lo).astype(jnp.int32)
    for d in range(32):
        reqs[d] = asked[d : d + 1, :]

    def tcopy(d):
        return rdma(reqs.at[d], rreqs.at[dp], ts.at[d], tr.at[dp], (seq, d))

    def tcopy_in(d):
        return rdma(reqs.at[d], rreqs.at[d], ts.at[d], tr.at[d], (seq, d))

    loop(1, 32, lambda k: tcopy(lax.rem(dp + k, 32)).start())
    c_lt = pltpu.make_async_copy(reqs.at[dp], rreqs.at[dp], lsem.at[5])
    c_lt.start()
    c_q.wait()
    n_out = rdma(q.at[pl.ds(0, 64)], qnext, ns, nr, prv)
    n_out.start()

    groups = nt(place, (marks * group).astype(BF))
    for d in range(32):
        place_d = ((d // 2) % 8) * 4 + (d // 16) * 2 + d % 2
        gcol[place_d // 4, (place_d % 4) * CAP : (place_d % 4 + 1) * CAP, :] = jnp.broadcast_to(
            groups[0:CAP, d : d + 1], (CAP, 128)
        )

    c_gm.wait()
    lane_low = iota((256, 128), 1) < 64
    for p in range(PAIRS):
        for src, dst in ((0, kbd), (1, vbd)):
            m = gm[src, :, p * 128 : (p + 1) * 128].astype(F32)
            dst[p, 0:256, :] = jnp.where(lane_low, m, 0.0).astype(BF)
            dst[p, 256:512, :] = jnp.where(lane_low, 0.0, m).astype(BF)

    y_send(KQ, 1, 8)

    c_lt.wait()
    loop(1, 32, lambda k: tcopy_in(lax.rem(dp + k, 32)).wait_recv())
    got = jnp.concatenate([rreqs[d] for d in range(32)], axis=0).astype(F32).T
    for d in range(32):
        icol[d] = jnp.broadcast_to(got[0:CAP, d : d + 1], (CAP, 128)).astype(jnp.int32)
    c_emb.wait()

    def dest(zz, j):
        return (j // 2) * 16 + zz * 2 + j % 2

    def rcopy(d, zz, j):
        return rdma(send.at[zz, j], rows.at[z, xl * 2 + c], rs.at[d], rr.at[dp], (seq, d))

    def rcopy_in(d, zz, j):
        return rdma(send.at[zz, j], rows.at[zz, j], rs.at[d], rr.at[d], (seq, d))

    def gather(u):
        for half in range(2):
            zz = lax.rem(z + offset_of(2 * u + half), 8)
            for j in range(4):
                idx = icol[dest(zz, j)]
                base = half * 192 + j * CAP
                for k in range(16):
                    onehot[base : base + CAP, k * 128 : (k + 1) * 128] = (
                        (iota((CAP, 128), 1) + k * 128) == idx
                    ).astype(BF)
        for n in range(7):
            got_rows = nn(onehot[...], emb[:, n * 128 : (n + 1) * 128]).astype(BF)
            for half in range(2):
                zz = lax.rem(z + offset_of(2 * u + half), 8)
                for j in range(4):
                    base = half * 192 + j * CAP
                    send[zz, j, :, n * 128 : (n + 1) * 128] = got_rows[base : base + CAP]
        for half in range(2):
            zz = lax.rem(z + offset_of(2 * u + half), 8)
            for j in range(4):
                d = dest(zz, j)

                @pl.when(d != dp)
                def _():
                    rcopy(d, zz, j).start()

                @pl.when(d == dp)
                def _():
                    pltpu.make_async_copy(send.at[zz, j], rows.at[zz, j], lsem.at[6]).start()

    loop(0, 2, gather)
    y_send(KK, 1, 4)
    loop(2, 4, gather)
    c_lq.wait()
    c_lk.wait()
    x_send(KQ, 0, 8)
    y_send(KK, 4, 8)
    x_send(KK, 0, 4)
    x_pass(KQ, 0, 8)
    s_wait(KQ)

    f = iota((448, 512), 0)
    perm = (iota((448, 512), 1) == f + 4 * lax.shift_right_logical(f * 2341, 16)).astype(BF)
    for which, dst in ((0, wqt), (2, wot)):
        for a in range(2):
            for d in range(16):
                pieces[d * 32 : (d + 1) * 32, :] = gq[a, d % 2, d // 2, which : which + 2].reshape(32, ENC)
            dst[a * 448 : (a + 1) * 448, :] = nn(perm, pieces[...]).astype(BF)

    memory_group = (lax.rem(iota((1, 512), 1), 256) // 64 + 1).astype(F32)

    def encode(u):
        for half in range(2):
            zz = lax.rem(z + offset_of(2 * u + half), 8)
            for j in range(4):
                d = dest(zz, j)

                @pl.when(d != dp)
                def _():
                    rcopy_in(d, zz, j).wait_recv()

                @pl.when(d == dp)
                def _():
                    pltpu.make_async_copy(send.at[zz, j], rows.at[zz, j], lsem.at[6]).wait()

        zs = [lax.rem(z + offset_of(2 * u + half), 8) for half in range(2)]
        wide = jnp.concatenate([rows[zz].reshape(192, ENC) for zz in zs], axis=0).astype(F32)
        gp = jnp.concatenate([gcol[zz] for zz in zs], axis=0)
        at = pl.multiple_of(u * UROWS, UROWS)
        gpos[pl.ds(at, UROWS), :] = gp
        inv = lax.rsqrt(jnp.mean(wide * wide, axis=-1, keepdims=True) + 1e-6)
        normed = (wide * inv).astype(BF)
        qenc[...] = nt(normed, wqt[...]).astype(BF)
        allowed = jnp.concatenate([gp] * 4, axis=1) == memory_group

        def pair(p):
            lanes = pl.ds(pl.multiple_of(p * 128, 128), 128)
            s = nt(qenc[:, lanes], kbd[p]) * 0.125
            s = jnp.where(allowed, s, NEG)
            ws = []
            for half in range(2):
                sh = s[:, half * 256 : (half + 1) * 256]
                e = jnp.exp(sh - jnp.max(sh, axis=-1, keepdims=True))
                ws.append((e * (1.0 / jnp.sum(e, axis=-1, keepdims=True))).astype(BF))
            w = jnp.concatenate(ws, axis=1)
            mixed[:, lanes] = nn(w, vbd[p]).astype(BF)

        loop(0, PAIRS, pair)
        xenc[u] = (wide + nt(mixed[...], wot[...])).astype(BF)

    def project(u):
        at = pl.multiple_of(u * UROWS, UROWS)

        def head(h):
            wk = gk[0, lax.rem(h, 2), h // 2].reshape(128, ENC)
            keys[h, pl.ds(at, UROWS), :] = nt(xenc[u], wk).astype(BF)
            wv = gk[1, lax.rem(h, 2), h // 2].reshape(128, ENC)
            valt[h, :, pl.ds(at, UROWS)] = nt(wv, xenc[u]).astype(BF)

        loop(0, HQ, head)

    encode(0)
    x_send(KK, 4, 8)
    encode(1)
    x_pass(KK, 0, 8)
    s_wait(KK)
    project(0)
    project(1)

    def last(u):
        encode(u)
        project(u)

    loop(2, 4, last)

    n_out.wait()
    first = iota((64, QW), 0) < 63
    mine = q[0:64, :]
    q[0:64, :] = jnp.where(first, qnext[...].astype(F32), mine.astype(F32)).astype(BF)
    r1 = iota((1, 256), 1) + 1
    qgroup = jnp.where(r1 < 64, 4, r1 // 64).astype(F32)
    scale = 1.0 / math.sqrt(HD)

    def attend(h):
        lanes = pl.ds(pl.multiple_of(h * HD, HD), HD)
        s = nt(keys[h], q[:, lanes]) * scale
        gp = gpos[...]
        s = jnp.where(jnp.concatenate([gp, gp], axis=1) == qgroup, s, NEG)
        e = jnp.exp(s - jnp.max(s, axis=0, keepdims=True))
        w = (e * (1.0 / jnp.sum(e, axis=0, keepdims=True))).astype(BF)
        outp[:, lanes] = nn(valt[h], w).T.astype(BF)

    def fcopy(k):
        p = pl.ds(k * 512, 512)
        return rdma(outp.at[pl.ds(0, 64), p], fin.at[:, p], fs.at[k], fr.at[k], nxt)

    for k in range(4):
        loop(4 * k, 4 * k + 4, attend)
        fcopy(k).start()

    drain(KQ)
    drain(KK)
    loop(1, 32, lambda k: tcopy(lax.rem(dp + k, 32)).wait_send())

    def rdone(i):
        zz = i // 4
        j = lax.rem(i, 4)
        d = (j // 2) * 16 + zz * 2 + lax.rem(j, 2)

        @pl.when(d != dp)
        def _():
            rcopy(d, zz, j).wait_send()

    loop(0, 32, rdone)

    out_ref[64:256, :] = outp[64:256, :]
    for k in range(4):
        fcopy(k).wait()
    keep = (iota((64, QW), 0) < 63).astype(F32)
    some = jnp.where(seq > 0, 1.0, 0.0).astype(F32)
    mine = outp[0:64, :].astype(F32)
    came = fin[...].astype(F32)
    out_ref[0:64, :] = jnp.where(keep > 0.5, came * some, mine).astype(BF)


def shards(queries, group_memory, nb_shard, nb_row, embed, w_query_enc, w_out_enc, w_kv_cca):
    own = nb_shard.reshape(1, TOK)
    rid = nb_row.reshape(1, TOK)
    gm = group_memory[0].transpose(1, 0, 2)
    D = pltpu.SemaphoreType.DMA
    vm = lambda *s: pltpu.VMEM(s, BF)
    any_ = pl.BlockSpec(memory_space=pl.ANY)
    here = pl.BlockSpec(memory_space=pltpu.VMEM)
    out = pl.pallas_call(
        body,
        out_shape=jax.ShapeDtypeStruct((256, QW), BF),
        in_specs=[here, here, any_, here, here, here, any_, any_],
        out_specs=here,
        scratch_shapes=[
            vm(2048, ENC), vm(2, 256, ENC), vm(256, QW), vm(4, 32, ENC), vm(4, 16, ENC),
            vm(2, 2, 8, 4, 32, ENC), vm(2, 2, 8, 4, 16, ENC),
            vm(8, 4, CAP, ENC), vm(8, 4, CAP, ENC), vm(UROWS, 2048),
            vm(HQ, SLOTS, HD), vm(HQ, HD, SLOTS), vm(ENC, ENC), vm(ENC, ENC), vm(512, ENC),
            vm(PAIRS, 512, 128), vm(PAIRS, 512, 128),
            pltpu.VMEM((32, 1, 128), jnp.int32), pltpu.VMEM((32, 1, 128), jnp.int32),
            pltpu.VMEM((32, CAP, 128), jnp.int32),
            pltpu.VMEM((8, 192, 128), F32), pltpu.VMEM((SLOTS, 128), F32),
            vm(UNITS, UROWS, ENC), vm(UROWS, ENC), vm(UROWS, ENC),
            vm(64, QW), vm(64, QW), vm(256, QW),
            D((7,)), D((8,)), D((8,)), D((8,)), D((8,)),
            D((8, 4)), D((8, 4)), D((8, 4)), D((8, 4)),
            D((8,)), D((8,)), D((8,)), D((8,)),
            D((2, 8)), D((2, 8)), D((2, 8)), D((2, 8)),
            D((32,)), D((32,)), D((32,)), D((32,)),
            D(()), D(()), D((4,)), D((4,)),
        ],
        compiler_params=pltpu.CompilerParams(
            collective_id=1, has_side_effects=True, vmem_limit_bytes=62 << 20
        ),
    )(own, rid, embed, w_query_enc.T, w_out_enc.T, w_kv_cca, gm, queries[0])
    return out[None]


def solution(mesh):
    in_specs = (
        P("dp", "seq", None),
        P("dp", "seq", None, None),
        P("dp", "seq", None, None, None),
        P("dp", "seq", None, None),
        P("dp", None),
        P(None, "dp"),
        P(None, "dp"),
        P(None, "dp"),
    )
    out_specs = P("dp", "seq", None)
    return jax.shard_map(shards, mesh=mesh, in_specs=in_specs, out_specs=out_specs, check_vma=False)
```

time: 381 us -> 182 us (0.48)
  waiting for transfers between devices: 182 us -> 0 us
  Pallas kernels: 0 us -> 174 us
  local copies, waits for them, and re-layouts: 80.2 us -> 4.5 us
  matrix products: 43.4 us -> 0 us
  other arithmetic: 34.7 us -> 0 us
  blocking collectives: 17 us -> 0 us
  between operations: 13.4 us -> 0.01 us
  starting transfers between devices: 9.49 us -> 0 us
    pallas_call x0 -> x1, Pallas kernels: none -> 174 us  [shards(): pl.pallas_call(body, out_shape=jax.ShapeDtypeStruct((256, QW), BF), in_sp...]
    all_gather x3 -> x0, waiting for transfers between devices: 134 us -> none  [the longest x1 71.3 us: shards(): lax.all_gather(w_out_enc, 'dp', axis=1, tiled=True)]
    ppermute x1 -> x0, waiting for transfers between devices: 46 us -> none  [shifted(): return lax.ppermute(array, axis, pairs)]
    dot_general x6 -> x0, matrix products: 43.4 us -> none  [the longest x1 16.9 us: shards(): jnp.dot(encoded, lax.all_gather(w_kv_cca, 'dp', axis=1, tiled=True), pref...]
    unnamed x23 -> x2, local copies, waits for them, and re-layouts: 33.3 us -> 4.5 us
    all_to_all x1 -> x0, blocking collectives: 17 us -> none  [shards(): lax.all_to_all(requests, 'dp', split_axis=0, concat_axis=0, tiled=True)]
    slice x5 -> x0, local copies, waits for them, and re-layouts: 16 us -> none  [the longest x1 10.2 us: shards(): stacked[:, :, :query_width].reshape(group_count + 1, span, HQ, HD)]
    gather x2 -> x0, local copies, waits for them, and re-layouts: 14.3 us -> none  [the longest x1 8.99 us: shards(): jnp.take(embed, lax.all_to_all(requests, 'dp', split_axis=0, concat_axis=...]
  transfers between devices with their start and end apart: 5 -> 0, of which waited for: 4 -> 0; matrix products, arithmetic and copies ran while one was open for 21% -> 0% of each run, Pallas kernels for 0% -> 0%
where the time goes in v1:
time: 182 us; the launch traced here: 179 us
  Pallas kernels  174 us (96%)
  local copies, waits for them, and re-layouts  4.5 us (2%)
    pallas_call x1, Pallas kernels, shards(): pl.pallas_call(body, out_shape=jax.ShapeDtypeStruct((256, QW), BF), in_sp...  174 us
    unnamed x2, local copies, waits for them, and re-layouts  4.5 us

profile of v1, /device:TPU:26, one launch (start us, length us, event | category | flops | bytes accessed | tf_op | source)
XLA Modules:
  0.0 178.9 jit_solution(1405662857758714698)
XLA Ops:
  0.0 2.2 %copy.11 = bf16[1,256,2,896]{3,1,2,0:T(8,128)(2,1)} copy(bf16[1,256,2,896]{3,2,1,0:T(2,128)(2,1)} %param.9) | data formatting | bytes 1835008 | tf_op args[1]
  2.2 174.4 %shard_map.82 = bf16[256,2048]{1,0:T(8,128)(2,1)} custom-call(s32[1,1024]{1,0:T(1,128)} %bitcast.16, s32[1,1024]{1,0:T(1,128)} %bitcast.17, bf16[2048,896]{1,0:T(8,128)(2,1)} %emb_hbm.1, bf16[28,896]{1,0:T(8,128)(2,1)} %bitcast.14, bf16[28,896]{1,0:T(8,128)(2,1)} %bitcast.15, bf16[896,128]{1,0:T(8,128)(2,1)} %wkv_ref.1, bf16[2,256,896]{2,1,0:T(8,128)(2,1)} %bitcast.12, ...), custom_call_target="tpu_custom_call" | custom-call | tf_op jit(solution)/shard_map/pallas_call | solution.py:466
  176.6 2.3 %copy.13 = bf16[1,256,2048]{2,1,0:T(8,128)(2,1)} copy(bf16[1,256,2048]{2,1,0:T(8,128)(2,1)} %bitcast.11) | data formatting | bytes 2097152

commit v2 on v1

--- a/solution.py
+++ b/solution.py
@@ -20,8 +20,8 @@
 PAIRS = 7
 UNITS = 4
 UROWS = 384
-SLOTS = 1536
 NEG = -1e30
+LOG2E = math.log2(math.e)
 
 
 def nt(a, b):
@@ -45,8 +45,8 @@
 def body(
     own_ref, rid_ref, emb_hbm, wq_ref, wo_ref, wkv_ref, gm_hbm, q_hbm,
     out_ref,
-    emb, gm, q, packk, packq, gk, gq, send, rows, onehot, keys, valt, wqt, wot, pieces,
-    kbd, vbd, reqs, rreqs, icol, gcol, gpos, xenc, qenc, mixed, qnext, fin, outp,
+    emb, gm, q, packk, packq, gk, gq, send, rows, onehot, keys, vals, wqt, wot, pieces,
+    kbd, vbdt, reqs, rreqs, icol, gcol, spos, xtok, qenc, mixed, qnext, qs, fin,
     lsem, zks, zkr, zqs, zqr, yks, ykr, yqs, yqr, xks, xkr, xqs, xqr, sks, skr, sqs, sqr,
     rs, rr, ts, tr, ns, nr, fs, fr,
 ):
@@ -96,8 +96,6 @@
     packq[2] = wo_ref[0:16, :]
     packq[3] = jnp.concatenate([wo_ref[16:28, :].astype(F32), zero4.astype(F32)], axis=0).astype(BF)
 
-    pl.semaphore_wait(bar, 38)
-
     def rdma(src, dst, s, r, dev):
         return pltpu.make_async_remote_copy(
             src_ref=src, dst_ref=dst, send_sem=s, recv_sem=r, device_id=dev, device_id_type=MESH
@@ -106,13 +104,29 @@
     KQ = (packq, gq, zqs, zqr, yqs, yqr, xqs, xqr, sqs, sqr)
     KK = (packk, gk, zks, zkr, yks, ykr, xks, xkr, sks, skr)
 
-    def zcopy(kind, zz):
+    def zcopy(kind, way, step):
         pack, g, s, r = kind[0], kind[1], kind[2], kind[3]
-        return rdma(pack.at[y], g.at[xl, c, z, y], s.at[zz], r.at[z], (seq, xl * 16 + zz * 2 + c))
-
-    def zcopy_in(kind, zz):
+        of = lax.rem(z - way * step + 8, 8)
+        to = lax.rem(z + way + 8, 8)
+        src = pack.at[y] if step == 0 else g.at[xl, c, of, y]
+        mark = step if way == 1 else 4 + step
+        return rdma(src, g.at[xl, c, of, y], s.at[mark], r.at[of], (seq, xl * 16 + to * 2 + c))
+
+    def zcopy_in(kind, way, step):
         pack, g, s, r = kind[0], kind[1], kind[2], kind[3]
-        return rdma(pack.at[y], g.at[xl, c, zz, y], s.at[zz], r.at[zz], (seq, xl * 16 + zz * 2 + c))
+        of = lax.rem(z - way * (step + 1) + 8, 8)
+        frm = lax.rem(z + way + 8, 8)
+        p = g.at[xl, c, of, y]
+        return rdma(p, p, s.at[of], r.at[of], (seq, xl * 16 + frm * 2 + c))
+
+    ZSTEPS = ((0, KQ, 1, 4), (1, KQ, -1, 3), (2, KK, -1, 4), (3, KK, 1, 3))
+
+    def z_step(step):
+        for n, kind, way, count in ZSTEPS:
+            if 0 < step <= count:
+                zcopy_in(kind, way, step - 1).wait_recv()
+            if step < count:
+                zcopy(kind, way, step).start()
 
     def ycopy(kind, zz, yy):
         g, s, r = kind[1], kind[4], kind[5]
@@ -151,17 +165,13 @@
 
         lax.fori_loop(lo, hi, step, 0)
 
-    def z_send(kind):
-        loop(1, 8, lambda k: zcopy(kind, lax.rem(z + k, 8)).start())
-
-    def y_send(kind, lo, hi):
+    def y_send(kind):
         def one(k):
             zz = lax.rem(z + k, 8)
-            zcopy_in(kind, zz).wait_recv()
             for j in range(1, 4):
                 ycopy(kind, zz, lax.rem(y + j, 4)).start()
 
-        loop(lo, hi, one)
+        loop(1, 8, one)
 
     def x_send(kind, lo, hi):
         def one(k):
@@ -209,18 +219,10 @@
 
         def two(k):
             zz = lax.rem(z + k, 8)
-            zcopy(kind, zz).wait_send()
             for j in range(1, 4):
                 ycopy(kind, zz, lax.rem(y + j, 4)).wait_send()
 
         loop(1, 8, two)
-
-    z_send(KQ)
-    z_send(KK)
-    c_lq = pltpu.make_async_copy(packq, gq.at[xl, c, z], lsem.at[3])
-    c_lk = pltpu.make_async_copy(packk, gk.at[xl, c, z], lsem.at[4])
-    c_lq.start()
-    c_lk.start()
 
     own = own_ref[...]
     marks = (iota((32, TOK), 0) == own).astype(F32)
@@ -250,13 +252,6 @@
     def tcopy_in(d):
         return rdma(reqs.at[d], rreqs.at[d], ts.at[d], tr.at[d], (seq, d))
 
-    loop(1, 32, lambda k: tcopy(lax.rem(dp + k, 32)).start())
-    c_lt = pltpu.make_async_copy(reqs.at[dp], rreqs.at[dp], lsem.at[5])
-    c_lt.start()
-    c_q.wait()
-    n_out = rdma(q.at[pl.ds(0, 64)], qnext, ns, nr, prv)
-    n_out.start()
-
     groups = nt(place, (marks * group).astype(BF))
     for d in range(32):
         place_d = ((d // 2) % 8) * 4 + (d // 16) * 2 + d % 2
@@ -264,15 +259,37 @@
             groups[0:CAP, d : d + 1], (CAP, 128)
         )
 
+    where = (
+        lax.rem(own // 2, 8) * 192 + ((own // 16) * 2 + lax.rem(own, 2)) * CAP + slot
+    ).astype(F32)
+    spos[...] = jnp.broadcast_to(where, (128, TOK)).T
+
     c_gm.wait()
     lane_low = iota((256, 128), 1) < 64
     for p in range(PAIRS):
-        for src, dst in ((0, kbd), (1, vbd)):
-            m = gm[src, :, p * 128 : (p + 1) * 128].astype(F32)
-            dst[p, 0:256, :] = jnp.where(lane_low, m, 0.0).astype(BF)
-            dst[p, 256:512, :] = jnp.where(lane_low, 0.0, m).astype(BF)
-
-    y_send(KQ, 1, 8)
+        f = slice(p * 128, (p + 1) * 128)
+        m = gm[:, 0, f].astype(F32)
+        kbd[p, 0:256, :] = jnp.where(lane_low, m, 0.0).astype(BF)
+        kbd[p, 256:512, :] = jnp.where(lane_low, 0.0, m).astype(BF)
+        m = gm[:, 1, f].astype(F32)
+        vbdt[p, :, 0:256] = jnp.where(lane_low, m, 0.0).T.astype(BF)
+        vbdt[p, :, 256:512] = jnp.where(lane_low, 0.0, m).T.astype(BF)
+    xtok[...] = jnp.zeros((TOK, ENC), BF)
+    c_q.wait()
+
+    pl.semaphore_wait(bar, 38)
+
+    loop(1, 32, lambda k: tcopy(lax.rem(dp + k, 32)).start())
+    c_lt = pltpu.make_async_copy(reqs.at[dp], rreqs.at[dp], lsem.at[5])
+    c_lt.start()
+    z_step(0)
+    c_lq = pltpu.make_async_copy(packq, gq.at[xl, c, z], lsem.at[3])
+    c_lk = pltpu.make_async_copy(packk, gk.at[xl, c, z], lsem.at[4])
+    c_lq.start()
+    c_lk.start()
+    n_out = rdma(q.at[pl.ds(0, 64)], qnext, ns, nr, prv)
+    n_out.start()
+    z_step(1)
 
     c_lt.wait()
     loop(1, 32, lambda k: tcopy_in(lax.rem(dp + k, 32)).wait_recv())
@@ -300,13 +317,14 @@
                     onehot[base : base + CAP, k * 128 : (k + 1) * 128] = (
                         (iota((CAP, 128), 1) + k * 128) == idx
                     ).astype(BF)
-        for n in range(7):
-            got_rows = nn(onehot[...], emb[:, n * 128 : (n + 1) * 128]).astype(BF)
-            for half in range(2):
-                zz = lax.rem(z + offset_of(2 * u + half), 8)
-                for j in range(4):
-                    base = half * 192 + j * CAP
-                    send[zz, j, :, n * 128 : (n + 1) * 128] = got_rows[base : base + CAP]
+        got_rows = nn(onehot[...], emb[...]).astype(BF)
+        for half in range(2):
+            zz = lax.rem(z + offset_of(2 * u + half), 8)
+            for j in range(4):
+                base = half * 192 + j * CAP
+                send[zz, j] = got_rows[base : base + CAP]
+
+    def row_send(u):
         for half in range(2):
             zz = lax.rem(z + offset_of(2 * u + half), 8)
             for j in range(4):
@@ -320,14 +338,31 @@
                 def _():
                     pltpu.make_async_copy(send.at[zz, j], rows.at[zz, j], lsem.at[6]).start()
 
-    loop(0, 2, gather)
-    y_send(KK, 1, 4)
-    loop(2, 4, gather)
+    z_step(2)
+    loop(0, 1, gather)
+    z_step(3)
+    loop(1, 2, gather)
+    z_step(4)
     c_lq.wait()
     c_lk.wait()
+    y_send(KQ)
+    y_send(KK)
+    loop(0, 2, row_send)
+
+    def gather_send(u):
+        gather(u)
+        row_send(u)
+
+    loop(2, 4, gather_send)
+
+    n_out.wait()
+    first = iota((64, QW), 0) < 63
+    head_rows = jnp.where(first, qnext[...].astype(F32), q[0:64, :].astype(F32)).astype(BF)
+    down = (iota((256, 256), 1) == lax.rem(iota((256, 256), 0) + 255, 256)).astype(BF)
+    qs[...] = nn(down, jnp.concatenate([head_rows, q[64:256, :]], axis=0)).astype(BF)
+
     x_send(KQ, 0, 8)
-    y_send(KK, 4, 8)
-    x_send(KK, 0, 4)
+    x_send(KK, 0, 8)
     x_pass(KQ, 0, 8)
     s_wait(KQ)
 
@@ -339,8 +374,6 @@
                 pieces[d * 32 : (d + 1) * 32, :] = gq[a, d % 2, d // 2, which : which + 2].reshape(32, ENC)
             dst[a * 448 : (a + 1) * 448, :] = nn(perm, pieces[...]).astype(BF)
 
-    memory_group = (lax.rem(iota((1, 512), 1), 256) // 64 + 1).astype(F32)
-
     def encode(u):
         for half in range(2):
             zz = lax.rem(z + offset_of(2 * u + half), 8)
@@ -357,78 +390,66 @@
 
         zs = [lax.rem(z + offset_of(2 * u + half), 8) for half in range(2)]
         wide = jnp.concatenate([rows[zz].reshape(192, ENC) for zz in zs], axis=0).astype(F32)
-        gp = jnp.concatenate([gcol[zz] for zz in zs], axis=0)
-        at = pl.multiple_of(u * UROWS, UROWS)
-        gpos[pl.ds(at, UROWS), :] = gp
+        gt = jnp.concatenate([gcol[zz] for zz in zs], axis=0).T[0:8]
+        bias = [
+            jnp.broadcast_to(jnp.where(gt[0:1] == float(m + 1), 0.0, NEG), (64, UROWS))
+            for m in range(4)
+        ]
+        bias = jnp.concatenate(bias * 2, axis=0)
         inv = lax.rsqrt(jnp.mean(wide * wide, axis=-1, keepdims=True) + 1e-6)
-        normed = (wide * inv).astype(BF)
-        qenc[...] = nt(normed, wqt[...]).astype(BF)
-        allowed = jnp.concatenate([gp] * 4, axis=1) == memory_group
-
-        def pair(p):
-            lanes = pl.ds(pl.multiple_of(p * 128, 128), 128)
-            s = nt(qenc[:, lanes], kbd[p]) * 0.125
-            s = jnp.where(allowed, s, NEG)
-            ws = []
-            for half in range(2):
-                sh = s[:, half * 256 : (half + 1) * 256]
-                e = jnp.exp(sh - jnp.max(sh, axis=-1, keepdims=True))
-                ws.append((e * (1.0 / jnp.sum(e, axis=-1, keepdims=True))).astype(BF))
-            w = jnp.concatenate(ws, axis=1)
-            mixed[:, lanes] = nn(w, vbd[p]).astype(BF)
-
-        loop(0, PAIRS, pair)
-        xenc[u] = (wide + nt(mixed[...], wot[...])).astype(BF)
-
-    def project(u):
-        at = pl.multiple_of(u * UROWS, UROWS)
-
-        def head(h):
-            wk = gk[0, lax.rem(h, 2), h // 2].reshape(128, ENC)
-            keys[h, pl.ds(at, UROWS), :] = nt(xenc[u], wk).astype(BF)
-            wv = gk[1, lax.rem(h, 2), h // 2].reshape(128, ENC)
-            valt[h, :, pl.ds(at, UROWS)] = nt(wv, xenc[u]).astype(BF)
-
-        loop(0, HQ, head)
-
-    encode(0)
-    x_send(KK, 4, 8)
-    encode(1)
+        qenc[...] = nt((wide * inv).astype(BF), wqt[...]).astype(BF)
+        for lo, hi in ((0, 4), (4, 7)):
+            scores = [nt(kbd[p], qenc[:, p * 128 : (p + 1) * 128]) for p in range(lo, hi)]
+            weights = []
+            for s in scores:
+                s = s * (0.125 * LOG2E) + bias
+                for half in range(2):
+                    sh = s[half * 256 : (half + 1) * 256]
+                    e = jnp.exp2(sh - jnp.max(sh, axis=0, keepdims=True))
+                    weights.append((e * (1.0 / jnp.sum(e, axis=0, keepdims=True))).astype(BF))
+            for p in range(lo, hi):
+                w = jnp.concatenate(weights[2 * (p - lo) : 2 * (p - lo) + 2], axis=0)
+                mixed[:, p * 128 : (p + 1) * 128] = nn(vbdt[p], w).T.astype(BF)
+        done = (wide + nt(mixed[...], wot[...])).astype(BF)
+        lane = iota((1, UROWS), 1)
+        want = jnp.where(lane < 192, zs[0] * 192 + lane, zs[1] * 192 + lane - 192).astype(F32)
+        move = (jnp.concatenate([spos[...]] * 3, axis=1) == want).astype(BF)
+        xtok[...] = xtok[...] + nn(move, done).astype(BF)
+
+    def project(lo, hi):
+        for dst, a in ((keys, 0), (vals, 1)):
+            for i in range(2):
+                w = gk[a, i].reshape(1024, ENC)
+                dst[lo:hi, i * 1024 : (i + 1) * 1024] = nt(xtok[lo:hi, :], w).astype(BF)
+
+    def feature(h):
+        return ((h % 2) * 8 + h // 2) * HD
+
+    def attend(b, at):
+        r = pl.ds(pl.multiple_of(b * 64, 64), 64)
+        kr = pl.ds(pl.multiple_of(lax.rem(b + 3, 4) * 256, 256), 256)
+        s = [
+            nt(qs[r, h * HD : (h + 1) * HD], keys[kr, feature(h) : feature(h) + HD])
+            for h in range(HQ)
+        ]
+        s = jnp.concatenate(s, axis=0) * (LOG2E / math.sqrt(HD))
+        e = jnp.exp2(s - jnp.max(s, axis=-1, keepdims=True))
+        w = (e * (1.0 / jnp.sum(e, axis=-1, keepdims=True))).astype(BF)
+        for h in range(HQ):
+            v = vals[kr, feature(h) : feature(h) + HD]
+            at[r, h * HD : (h + 1) * HD] = nn(w[h * 64 : (h + 1) * 64], v).astype(BF)
+
+    loop(0, 3, encode)
     x_pass(KK, 0, 8)
+    loop(3, 4, encode)
     s_wait(KK)
-    project(0)
-    project(1)
-
-    def last(u):
-        encode(u)
-        project(u)
-
-    loop(2, 4, last)
-
-    n_out.wait()
-    first = iota((64, QW), 0) < 63
-    mine = q[0:64, :]
-    q[0:64, :] = jnp.where(first, qnext[...].astype(F32), mine.astype(F32)).astype(BF)
-    r1 = iota((1, 256), 1) + 1
-    qgroup = jnp.where(r1 < 64, 4, r1 // 64).astype(F32)
-    scale = 1.0 / math.sqrt(HD)
-
-    def attend(h):
-        lanes = pl.ds(pl.multiple_of(h * HD, HD), HD)
-        s = nt(keys[h], q[:, lanes]) * scale
-        gp = gpos[...]
-        s = jnp.where(jnp.concatenate([gp, gp], axis=1) == qgroup, s, NEG)
-        e = jnp.exp(s - jnp.max(s, axis=0, keepdims=True))
-        w = (e * (1.0 / jnp.sum(e, axis=0, keepdims=True))).astype(BF)
-        outp[:, lanes] = nn(valt[h], w).T.astype(BF)
-
-    def fcopy(k):
-        p = pl.ds(k * 512, 512)
-        return rdma(outp.at[pl.ds(0, 64), p], fin.at[:, p], fs.at[k], fr.at[k], nxt)
-
-    for k in range(4):
-        loop(4 * k, 4 * k + 4, attend)
-        fcopy(k).start()
+
+    project(768, 1024)
+    attend(0, out_ref)
+    f_out = rdma(out_ref.at[pl.ds(0, 64)], fin, fs, fr, nxt)
+    f_out.start()
+    project(0, 768)
+    loop(1, 4, lambda b: attend(b, out_ref))
 
     drain(KQ)
     drain(KK)
@@ -445,20 +466,23 @@
 
     loop(0, 32, rdone)
 
-    out_ref[64:256, :] = outp[64:256, :]
-    for k in range(4):
-        fcopy(k).wait()
-    keep = (iota((64, QW), 0) < 63).astype(F32)
-    some = jnp.where(seq > 0, 1.0, 0.0).astype(F32)
-    mine = outp[0:64, :].astype(F32)
-    came = fin[...].astype(F32)
-    out_ref[0:64, :] = jnp.where(keep > 0.5, came * some, mine).astype(BF)
+    for n, kind, way, count in ZSTEPS:
+        for step in range(count):
+            zcopy(kind, way, step).wait_send()
+    f_out.wait()
+    came = jnp.where(seq > 0, 1.0, 0.0).astype(F32) * fin[...].astype(F32)
+    mine = out_ref[0:64, :].astype(F32)
+    out_ref[0:64, :] = jnp.where(iota((64, QW), 0) < 1, mine, came).astype(BF)
+
+
+def row_up(in_ref, out_ref):
+    up = (iota((256, 256), 1) == lax.rem(iota((256, 256), 0) + 1, 256)).astype(BF)
+    out_ref[...] = nn(up, in_ref[...]).astype(BF)
 
 
 def shards(queries, group_memory, nb_shard, nb_row, embed, w_query_enc, w_out_enc, w_kv_cca):
     own = nb_shard.reshape(1, TOK)
     rid = nb_row.reshape(1, TOK)
-    gm = group_memory[0].transpose(1, 0, 2)
     D = pltpu.SemaphoreType.DMA
     vm = lambda *s: pltpu.VMEM(s, BF)
     any_ = pl.BlockSpec(memory_space=pl.ANY)
@@ -469,27 +493,35 @@
         in_specs=[here, here, any_, here, here, here, any_, any_],
         out_specs=here,
         scratch_shapes=[
-            vm(2048, ENC), vm(2, 256, ENC), vm(256, QW), vm(4, 32, ENC), vm(4, 16, ENC),
+            vm(2048, ENC), vm(256, 2, ENC), vm(256, QW), vm(4, 32, ENC), vm(4, 16, ENC),
             vm(2, 2, 8, 4, 32, ENC), vm(2, 2, 8, 4, 16, ENC),
             vm(8, 4, CAP, ENC), vm(8, 4, CAP, ENC), vm(UROWS, 2048),
-            vm(HQ, SLOTS, HD), vm(HQ, HD, SLOTS), vm(ENC, ENC), vm(ENC, ENC), vm(512, ENC),
-            vm(PAIRS, 512, 128), vm(PAIRS, 512, 128),
+            vm(TOK, QW), vm(TOK, QW), vm(ENC, ENC), vm(ENC, ENC), vm(512, ENC),
+            vm(PAIRS, 512, 128), vm(PAIRS, 128, 512),
             pltpu.VMEM((32, 1, 128), jnp.int32), pltpu.VMEM((32, 1, 128), jnp.int32),
             pltpu.VMEM((32, CAP, 128), jnp.int32),
-            pltpu.VMEM((8, 192, 128), F32), pltpu.VMEM((SLOTS, 128), F32),
-            vm(UNITS, UROWS, ENC), vm(UROWS, ENC), vm(UROWS, ENC),
-            vm(64, QW), vm(64, QW), vm(256, QW),
+            pltpu.VMEM((8, 192, 128), F32), pltpu.VMEM((TOK, 128), F32),
+            vm(TOK, ENC), vm(UROWS, ENC), vm(UROWS, ENC),
+            vm(64, QW), vm(256, QW), vm(64, QW),
             D((7,)), D((8,)), D((8,)), D((8,)), D((8,)),
             D((8, 4)), D((8, 4)), D((8, 4)), D((8, 4)),
             D((8,)), D((8,)), D((8,)), D((8,)),
             D((2, 8)), D((2, 8)), D((2, 8)), D((2, 8)),
             D((32,)), D((32,)), D((32,)), D((32,)),
-            D(()), D(()), D((4,)), D((4,)),
+            D(()), D(()), D(()), D(()),
         ],
         compiler_params=pltpu.CompilerParams(
             collective_id=1, has_side_effects=True, vmem_limit_bytes=62 << 20
         ),
-    )(own, rid, embed, w_query_enc.T, w_out_enc.T, w_kv_cca, gm, queries[0])
+    )(own, rid, embed, w_query_enc.T, w_out_enc.T, w_kv_cca, group_memory[0], queries[0])
+    block = pl.BlockSpec((256, 512), lambda i: (0, i))
+    out = pl.pallas_call(
+        row_up,
+        grid=(4,),
+        out_shape=jax.ShapeDtypeStruct((256, QW), BF),
+        in_specs=[block],
+        out_specs=block,
+    )(out)
     return out[None]
 
 

time: 182 us -> 121 us (0.66)
  Pallas kernels: 174 us -> 119 us
  local copies, waits for them, and re-layouts: 4.5 us -> 0 us
    pallas_call x1, Pallas kernels: 174 us -> 116 us  [shards(): pl.pallas_call(body, out_shape=jax.ShapeDtypeStruct((256, QW), BF), in_sp...]
    unnamed x2 -> x0, local copies, waits for them, and re-layouts: 4.5 us -> none
    pallas_call x0 -> x1, Pallas kernels: none -> 3.79 us  [shards(): pl.pallas_call(row_up, grid=(4,), out_shape=jax.ShapeDtypeStruct((256, QW...]
where the time goes in v2:
time: 121 us; the launch traced here: 119 us
  Pallas kernels  119 us (98%)
    pallas_call x1, Pallas kernels, shards(): pl.pallas_call(body, out_shape=jax.ShapeDtypeStruct((256, QW), BF), in_sp...  116 us
    pallas_call x1, Pallas kernels, shards(): pl.pallas_call(row_up, grid=(4,), out_shape=jax.ShapeDtypeStruct((256, QW...  3.79 us

profile of v2, /device:TPU:26, one launch (start us, length us, event | category | flops | bytes accessed | tf_op | source)
XLA Modules:
  0.0 119.3 jit_solution(14050184985832416849)
XLA Ops:
  0.0 115.5 %shard_map.82.in_ref = bf16[256,2048]{1,0:T(8,128)(2,1)} custom-call(s32[1,1024]{1,0:T(1,128)} %bitcast.11, s32[1,1024]{1,0:T(1,128)} %bitcast.12, bf16[2048,896]{1,0:T(8,128)(2,1)} %emb_hbm.1, bf16[28,896]{1,0:T(8,128)(2,1)} %bitcast.9, bf16[28,896]{1,0:T(8,128)(2,1)} %bitcast.10, bf16[896,128]{1,0:T(8,128)(2,1)} %wkv_ref.1, bf16[256,2,896]{2,1,0:T(2,128)(2,1)} %bitcast.8, ...), custom_call_target="tpu_custom_call" | custom-call | tf_op jit(solution)/shard_map/pallas_call | solution.py:490
  115.5 3.8 %shard_map.83 = bf16[256,2048]{1,0:T(8,128)(2,1)} custom-call(bf16[256,2048]{1,0:T(8,128)(2,1)} %shard_map.82.in_ref), custom_call_target="tpu_custom_call" | custom-call | tf_op jit(solution)/shard_map/pallas_call | solution.py:518

commit v3 on v2

--- a/solution.py
+++ b/solution.py
@@ -46,7 +46,7 @@
     own_ref, rid_ref, emb_hbm, wq_ref, wo_ref, wkv_ref, gm_hbm, q_hbm,
     out_ref,
     emb, gm, q, packk, packq, gk, gq, send, rows, onehot, keys, vals, wqt, wot, pieces,
-    kbd, vbdt, reqs, rreqs, icol, gcol, spos, xtok, qenc, mixed, qnext, qs, fin,
+    kbd, vbdt, reqs, rreqs, icol, gcol, spos, xtok, qenc, mixed, qnext, qs, fin, outp,
     lsem, zks, zkr, zqs, zqr, yks, ykr, yqs, yqr, xks, xkr, xqs, xqr, sks, skr, sqs, sqr,
     rs, rr, ts, tr, ns, nr, fs, fr,
 ):
@@ -165,13 +165,13 @@
 
         lax.fori_loop(lo, hi, step, 0)
 
-    def y_send(kind):
+    def y_send(kind, lo, hi):
         def one(k):
             zz = lax.rem(z + k, 8)
             for j in range(1, 4):
                 ycopy(kind, zz, lax.rem(y + j, 4)).start()
 
-        loop(1, 8, one)
+        loop(lo, hi, one)
 
     def x_send(kind, lo, hi):
         def one(k):
@@ -182,11 +182,11 @@
                 for j in range(1, 4):
                     ycopy_in(kind, zz, lax.rem(y + j, 4)).wait_recv()
 
-            @pl.when(lax.rem(zz, 4) == 0)
+            @pl.when(lax.rem(zz, 3) == 0)
             def _():
                 xcopy(kind, zz, partner).start()
 
-            @pl.when(lax.rem(zz, 4) != 0)
+            @pl.when(lax.rem(zz, 3) != 0)
             def _():
                 xcopy(kind, zz, wrap).start()
 
@@ -209,7 +209,7 @@
 
         loop(0, 8, one)
 
-    def drain(kind):
+    def drain_x(kind):
         def one(zz):
             xcopy(kind, zz, partner).wait_send()
             for a in range(2):
@@ -217,12 +217,13 @@
 
         loop(0, 8, one)
 
-        def two(k):
+    def drain_y(kind):
+        def one(k):
             zz = lax.rem(z + k, 8)
             for j in range(1, 4):
                 ycopy(kind, zz, lax.rem(y + j, 4)).wait_send()
 
-        loop(1, 8, two)
+        loop(1, 8, one)
 
     own = own_ref[...]
     marks = (iota((32, TOK), 0) == own).astype(F32)
@@ -345,8 +346,7 @@
     z_step(4)
     c_lq.wait()
     c_lk.wait()
-    y_send(KQ)
-    y_send(KK)
+    y_send(KQ, 1, 8)
     loop(0, 2, row_send)
 
     def gather_send(u):
@@ -354,6 +354,7 @@
         row_send(u)
 
     loop(2, 4, gather_send)
+    y_send(KK, 1, 5)
 
     n_out.wait()
     first = iota((64, QW), 0) < 63
@@ -362,8 +363,10 @@
     qs[...] = nn(down, jnp.concatenate([head_rows, q[64:256, :]], axis=0)).astype(BF)
 
     x_send(KQ, 0, 8)
-    x_send(KK, 0, 8)
+    y_send(KK, 5, 8)
+    x_send(KK, 0, 5)
     x_pass(KQ, 0, 8)
+    x_send(KK, 5, 8)
     s_wait(KQ)
 
     f = iota((448, 512), 0)
@@ -441,19 +444,24 @@
 
     loop(0, 3, encode)
     x_pass(KK, 0, 8)
+    drain_y(KQ)
+    drain_y(KK)
+    drain_x(KQ)
+    loop(1, 32, lambda k: tcopy(lax.rem(dp + k, 32)).wait_send())
+    for n, kind, way, count in ZSTEPS:
+        for step in range(count):
+            zcopy(kind, way, step).wait_send()
     loop(3, 4, encode)
     s_wait(KK)
 
     project(768, 1024)
-    attend(0, out_ref)
-    f_out = rdma(out_ref.at[pl.ds(0, 64)], fin, fs, fr, nxt)
+    attend(0, outp)
+    f_out = rdma(outp.at[pl.ds(0, 64)], fin, fs, fr, nxt)
     f_out.start()
     project(0, 768)
-    loop(1, 4, lambda b: attend(b, out_ref))
-
-    drain(KQ)
-    drain(KK)
-    loop(1, 32, lambda k: tcopy(lax.rem(dp + k, 32)).wait_send())
+    loop(1, 4, lambda b: attend(b, outp))
+
+    drain_x(KK)
 
     def rdone(i):
         zz = i // 4
@@ -466,18 +474,12 @@
 
     loop(0, 32, rdone)
 
-    for n, kind, way, count in ZSTEPS:
-        for step in range(count):
-            zcopy(kind, way, step).wait_send()
     f_out.wait()
     came = jnp.where(seq > 0, 1.0, 0.0).astype(F32) * fin[...].astype(F32)
-    mine = out_ref[0:64, :].astype(F32)
-    out_ref[0:64, :] = jnp.where(iota((64, QW), 0) < 1, mine, came).astype(BF)
-
-
-def row_up(in_ref, out_ref):
+    mine = outp[0:64, :].astype(F32)
+    top = jnp.where(iota((64, QW), 0) < 1, mine, came).astype(BF)
     up = (iota((256, 256), 1) == lax.rem(iota((256, 256), 0) + 1, 256)).astype(BF)
-    out_ref[...] = nn(up, in_ref[...]).astype(BF)
+    out_ref[...] = nn(up, jnp.concatenate([top, outp[64:256, :]], axis=0)).astype(BF)
 
 
 def shards(queries, group_memory, nb_shard, nb_row, embed, w_query_enc, w_out_enc, w_kv_cca):
@@ -502,7 +504,7 @@
             pltpu.VMEM((32, CAP, 128), jnp.int32),
             pltpu.VMEM((8, 192, 128), F32), pltpu.VMEM((TOK, 128), F32),
             vm(TOK, ENC), vm(UROWS, ENC), vm(UROWS, ENC),
-            vm(64, QW), vm(256, QW), vm(64, QW),
+            vm(64, QW), vm(256, QW), vm(64, QW), vm(256, QW),
             D((7,)), D((8,)), D((8,)), D((8,)), D((8,)),
             D((8, 4)), D((8, 4)), D((8, 4)), D((8, 4)),
             D((8,)), D((8,)), D((8,)), D((8,)),
@@ -514,14 +516,6 @@
             collective_id=1, has_side_effects=True, vmem_limit_bytes=62 << 20
         ),
     )(own, rid, embed, w_query_enc.T, w_out_enc.T, w_kv_cca, group_memory[0], queries[0])
-    block = pl.BlockSpec((256, 512), lambda i: (0, i))
-    out = pl.pallas_call(
-        row_up,
-        grid=(4,),
-        out_shape=jax.ShapeDtypeStruct((256, QW), BF),
-        in_specs=[block],
-        out_specs=block,
-    )(out)
     return out[None]
 
 

time: 121 us -> 120 us (level)
  Pallas kernels: 119 us -> 116 us
  local copies, waits for them, and re-layouts: 0 us -> 2.3 us
    pallas_call x1 -> x0, Pallas kernels: 3.79 us -> none  [shards(): pl.pallas_call(row_up, grid=(4,), out_shape=jax.ShapeDtypeStruct((256, QW...]
    unnamed x0 -> x1, local copies, waits for them, and re-layouts: none -> 2.3 us
where the time goes in v3:
time: 120 us; the launch traced here: 118 us
  Pallas kernels  116 us (97%)
  local copies, waits for them, and re-layouts  2.3 us (2%)
    pallas_call x1, Pallas kernels, shards(): pl.pallas_call(body, out_shape=jax.ShapeDtypeStruct((256, QW), BF), in_sp...  116 us

profile of v3, /device:TPU:26, one launch (start us, length us, event | category | flops | bytes accessed | tf_op | source)
XLA Modules:
  0.0 118.0 jit_solution(14968741157345669142)
XLA Ops:
  0.0 115.7 %shard_map.82 = bf16[256,2048]{1,0:T(8,128)(2,1)} custom-call(s32[1,1024]{1,0:T(1,128)} %bitcast.12, s32[1,1024]{1,0:T(1,128)} %bitcast.13, bf16[2048,896]{1,0:T(8,128)(2,1)} %emb_hbm.1, bf16[28,896]{1,0:T(8,128)(2,1)} %bitcast.10, bf16[28,896]{1,0:T(8,128)(2,1)} %bitcast.11, bf16[896,128]{1,0:T(8,128)(2,1)} %wkv_ref.1, bf16[256,2,896]{2,1,0:T(2,128)(2,1)} %bitcast.9, ...), custom_call_target="tpu_custom_call" | custom-call | tf_op jit(solution)/shard_map/pallas_call | solution.py:492
  115.7 2.3 %copy.10 = bf16[1,256,2048]{2,1,0:T(8,128)(2,1)} copy(bf16[1,256,2048]{2,1,0:T(8,128)(2,1)} %bitcast.7) | data formatting | bytes 2097152

commit v4 on v3

--- a/solution.py
+++ b/solution.py
@@ -37,9 +37,11 @@
 
 
 def offset_of(k):
-    base = 4 - (k + 1) // 2
+    a = lax.rem(k // 2, 2)
+    b = k // 4
     odd = lax.rem(k, 2)
-    return lax.rem(odd * base + (1 - odd) * (8 - base), 8)
+    base = 3 + a - b - 2 * a * b
+    return (1 - odd) * base + odd * lax.rem(8 - base - 4 * a * (1 - b), 8)
 
 
 def body(
@@ -344,10 +346,10 @@
     z_step(3)
     loop(1, 2, gather)
     z_step(4)
+    loop(0, 2, row_send)
     c_lq.wait()
     c_lk.wait()
     y_send(KQ, 1, 8)
-    loop(0, 2, row_send)
 
     def gather_send(u):
         gather(u)

time: 120 us -> 112 us (0.933)
  Pallas kernels: 116 us -> 108 us
    pallas_call x1, Pallas kernels: 116 us -> 108 us  [shards(): pl.pallas_call(body, out_shape=jax.ShapeDtypeStruct((256, QW), BF), in_sp...]
where the time goes in v4:
time: 112 us; the launch traced here: 111 us
  Pallas kernels  108 us (96%)
  local copies, waits for them, and re-layouts  2.3 us (2%)
    pallas_call x1, Pallas kernels, shards(): pl.pallas_call(body, out_shape=jax.ShapeDtypeStruct((256, QW), BF), in_sp...  108 us
    unnamed x1, local copies, waits for them, and re-layouts  2.3 us

profile of v4, /device:TPU:26, one launch (start us, length us, event | category | flops | bytes accessed | tf_op | source)
XLA Modules:
  0.0 110.7 jit_solution(18034645621677024647)
XLA Ops:
  0.0 108.4 %shard_map.82 = bf16[256,2048]{1,0:T(8,128)(2,1)} custom-call(s32[1,1024]{1,0:T(1,128)} %bitcast.12, s32[1,1024]{1,0:T(1,128)} %bitcast.13, bf16[2048,896]{1,0:T(8,128)(2,1)} %emb_hbm.1, bf16[28,896]{1,0:T(8,128)(2,1)} %bitcast.10, bf16[28,896]{1,0:T(8,128)(2,1)} %bitcast.11, bf16[896,128]{1,0:T(8,128)(2,1)} %wkv_ref.1, bf16[256,2,896]{2,1,0:T(2,128)(2,1)} %bitcast.9, ...), custom_call_target="tpu_custom_call" | custom-call | tf_op jit(solution)/shard_map/pallas_call | solution.py:494
  108.4 2.3 %copy.10 = bf16[1,256,2048]{2,1,0:T(8,128)(2,1)} copy(bf16[1,256,2048]{2,1,0:T(8,128)(2,1)} %bitcast.7) | data formatting | bytes 2097152
